TPU v7x, 512 devices: a whole 4x4x16 slice. The times are simulated.
512 devices in a mesh: segment: 8 (over y, core), rows: 16 (over z), dp: 4 (over x).
Axes of the slice: x: 4, y: 4, z: 16, core: 2. Of those that a mesh axis runs over, the one named last changes fastest.
Arguments:
- clips: bfloat16 [4, 4, 4, 128, 8, 128], P(None, 'dp', None, 'rows'), may hold values from -80 to 80
- lengths: int32 [4, 4], P(None, 'dp'), may hold values from 1 to 4, as said below
- conv_weight: bfloat16 [8, 3456, 128], P('segment'), may hold values from -0.109375 to 0.109375
- norm_gain: float32 [8, 128], P('segment'), may hold values from 0.5 to 2
- norm_shift: float32 [8, 128], P('segment'), may hold values from -1 to 1
- conv_bias: float32 [8, 128], P('segment'), may hold values from -3 to 3
- cotangent: bfloat16 [8, 4, 4, 4, 128, 8, 128], P('segment', None, 'dp', None, 'rows'), may hold values from -6 to 6
Outputs:
- stash: bfloat16 [8, 4, 4, 4, 128, 8, 128], P('segment', None, 'dp', None, 'rows')
- weight_grad: float32 [8, 3456, 128], P('segment')
Inputs may be any that keep to these rules, and one draw needn't show every extreme that they name: lengths[m, clip] real frames lead each clip; the frames after them are padding; some clip has all 4 frames.
All inputs are finite; a program needn't handle non-finite values.
Results may differ from a plain program's by a relative error of at most 0.009.
Values may be sent and summed in bfloat16 or wider, within the bound.
A program may use at most 64 MiB of HBM per device.

v0:
```python
import math
import jax
import jax.numpy as jnp
from jax import lax
from jax.sharding import PartitionSpec as P

GROUPS = 32
eps = 1e-06


def extended_2(cells, sides, width):
    for axis, dim in sides:
        count = lax.axis_size(axis)
        ends = count - 1
        head = lax.slice_in_dim(cells, 0, width, axis=dim)
        tail = lax.slice_in_dim(cells, cells.shape[dim] - width, cells.shape[dim], axis=dim)
        cells = jnp.concatenate(
            [
                lax.ppermute(tail, axis, [(i, (i + 1) % count) for i in range(ends)]),
                cells,
                lax.ppermute(head, axis, [((i + 1) % count, i) for i in range(ends)]),
            ],
            axis=dim,
        )
    return cells


def passed_along(block, axis, distance):
    devices = range(lax.axis_size(axis))
    route = [(i - distance, i) for i in devices if i - distance in devices]
    return lax.ppermute(block, axis, route)


def statistics(values, frame_mask, length, height):
    clip_count, frames, rows_here, cols, chans = values.shape
    sub = chans // GROUPS
    grouped = values.reshape(clip_count, frames, rows_here, cols, GROUPS, sub)
    mask_six = frame_mask[:, :, :, :, :, None]
    count = (length * (height * cols * sub)).astype(jnp.float32)[:, None]
    total = lax.psum(jnp.sum(grouped * mask_six, axis=(1, 2, 3, 5)), "rows")
    mean = total / count
    centered = grouped - mean[:, None, None, None, :, None]
    spread = lax.psum(jnp.sum(centered * centered * mask_six, axis=(1, 2, 3, 5)), "rows")
    var = spread / count
    rstd = lax.rsqrt(var + eps)
    mean_chan = jnp.repeat(mean, sub, axis=-1)[:, None, None, None, :]
    rstd_chan = jnp.repeat(rstd, sub, axis=-1)[:, None, None, None, :]
    return (mean_chan, rstd_chan)


def block(current, length, weight, gain, shift, bias, height):
    clip_count, frames, rows_here, cols, chans = current.shape
    values = current.astype(jnp.float32)
    frame_mask = (jnp.arange(frames)[None, :] < length[:, None]).astype(jnp.float32)[
        :, :, None, None, None
    ]
    mean_chan, rstd_chan = statistics(values, frame_mask, length, height)
    hidden = jax.nn.silu((values - mean_chan) * rstd_chan * gain + shift).astype(jnp.bfloat16)
    extended = extended_2(hidden, (("rows", 2),), 1)
    padded = jnp.pad(extended, ((0, 0), (0, 0), (0, 0), (1, 1), (0, 0)))
    padded = jnp.concatenate([padded[:, :1], padded[:, :1], padded], axis=1)
    pieces = []
    for tap_t in range(3):
        for tap_h in range(3):
            for tap_w in range(3):
                pieces.append(
                    padded[
                        :,
                        tap_t : tap_t + frames,
                        tap_h : tap_h + rows_here,
                        tap_w : tap_w + cols,
                        :,
                    ]
                )
    patches = jnp.concatenate(pieces, axis=-1).reshape(-1, 27 * chans)
    conv = jnp.dot(patches, weight, preferred_element_type=jnp.float32).reshape(values.shape)
    result = ((values + conv + bias) * frame_mask).astype(jnp.bfloat16)
    return (result, patches, frame_mask.astype(jnp.bfloat16))


def per_device(clips, lengths, conv_weight, norm_gain, norm_shift, conv_bias, cotangent):
    segments = lax.axis_size("segment")
    segment_id = lax.axis_index("segment")
    micro = clips.shape[0]
    frames = clips.shape[2]
    cols = clips.shape[4]
    chans = clips.shape[5]
    height = clips.shape[3] * lax.axis_size("rows")
    weight = conv_weight[0]
    gain = norm_gain[0]
    shift = norm_shift[0]
    bias = conv_bias[0]
    cot_all = cotangent[0]
    total_cells = micro * clips.shape[1] * lax.axis_size("dp") * frames * height * cols
    factor = 1.0 / math.sqrt(total_cells)

    def tick(step, carry):
        arrived, stash, grads = carry
        which = step - segment_id
        valid = (which >= 0) & (which < micro)
        slot = jnp.clip(which, 0, micro - 1)
        fresh = lax.dynamic_index_in_dim(
            clips, jnp.clip(step, 0, micro - 1).astype(jnp.int32), 0, keepdims=False
        )
        current = jnp.where(segment_id == 0, fresh, arrived)
        length = lax.dynamic_index_in_dim(lengths, slot, 0, keepdims=False)
        result, patches, mask_five = block(current, length, weight, gain, shift, bias, height)
        cot_now = lax.dynamic_index_in_dim(cot_all, slot, 0, keepdims=False)
        masked = (cot_now * mask_five).reshape(-1, chans)
        term = lax.dot_general(
            patches, masked, (((0,), (0,)), ((), ())), preferred_element_type=jnp.float32
        )
        grads = grads + jnp.where(valid, term, 0.0)
        previous = lax.dynamic_index_in_dim(stash, slot, 0, keepdims=False)
        stash = lax.dynamic_update_index_in_dim(stash, jnp.where(valid, result, previous), slot, 0)
        arrived = passed_along(result, "segment", 1)
        return (arrived, stash, grads)

    start = (
        jnp.zeros(clips.shape[1:], jnp.bfloat16),
        jnp.zeros(clips.shape, jnp.bfloat16),
        jnp.zeros((27 * chans, chans), jnp.float32),
    )
    arrived, stash, grads = lax.fori_loop(0, micro + segments - 1, tick, start)
    grads = lax.psum(grads, ("rows", "dp")) * factor
    return (stash[None], grads[None])


def solution(mesh):
    in_specs = (
        P(None, "dp", None, "rows", None, None),
        P(None, "dp"),
        P("segment", None, None),
        P("segment", None),
        P("segment", None),
        P("segment", None),
        P("segment", None, "dp", None, "rows", None, None),
    )
    out_specs = (P("segment", None, "dp", None, "rows", None, None), P("segment", None, None))
    return jax.shard_map(
        per_device, mesh=mesh, in_specs=in_specs, out_specs=out_specs, check_vma=False
    )
```

profile of v0, /device:TPU:8, one launch (start us, length us, event | category | flops | bytes accessed | tf_op | source)
XLA Modules:
  0.0 1160.9 jit_solution(13718055022507466365)
XLA Ops:
  7.3 867.2 %while.20 = (s32[]{:T(128)}, bf16[1,4,8,8,128]{4,3,2,1,0:T(8,128)(2,1)S(1)}, bf16[4,1,4,8,8,128]{5,4,3,2,1,0:T(8,128)(2,1)S(1)}, f32[3456,128]{1,0:T(8,128)S(1)}...) while((s32[]{:T(128)}, ...), condition=%wide.region_7.8_spmd.clone, body=%wide.region_0.7_spmd.clone.sunk | while | flops 457701504 | bytes 18060908 | solution.py:124
  10.4 36.5 %psum.40 = f32[1,32]{1,0:T(1,128)S(1)} all-reduce(f32[1,32]{1,0:T(1,128)S(1)} %bitcast.110), channel_id=1, replica_groups=mesh['segment'=8,'rows'=16,'dp'=4] {'rows'}, use_global_device_ids=true, to_apply=%region_3.3 | all-reduce | flops 32 | bytes 256 | tf_op jit(solution)/shard_map/while/body/eval_jaxpr/psum | solution.py:40
  48.0 27.0 %psum.41 = f32[1,32]{1,0:T(1,128)S(1)} all-reduce(f32[1,32]{1,0:T(1,128)S(1)} %bitcast.109), channel_id=1, replica_groups=mesh['segment'=8,'rows'=16,'dp'=4] {'rows'}, use_global_device_ids=true, to_apply=%region_6.6 | all-reduce | flops 32 | bytes 256 | tf_op jit(solution)/shard_map/while/body/eval_jaxpr/psum | solution.py:43
  94.2 30.5 %psum.40 = f32[1,32]{1,0:T(1,128)S(1)} all-reduce(f32[1,32]{1,0:T(1,128)S(1)} %bitcast.110), channel_id=1, replica_groups=mesh['segment'=8,'rows'=16,'dp'=4] {'rows'}, use_global_device_ids=true, to_apply=%region_3.3 | all-reduce | flops 32 | bytes 256 | tf_op jit(solution)/shard_map/while/body/eval_jaxpr/psum | solution.py:40
  125.8 29.1 %psum.41 = f32[1,32]{1,0:T(1,128)S(1)} all-reduce(f32[1,32]{1,0:T(1,128)S(1)} %bitcast.109), channel_id=1, replica_groups=mesh['segment'=8,'rows'=16,'dp'=4] {'rows'}, use_global_device_ids=true, to_apply=%region_6.6 | all-reduce | flops 32 | bytes 256 | tf_op jit(solution)/shard_map/while/body/eval_jaxpr/psum | solution.py:43
  174.0 29.3 %psum.40 = f32[1,32]{1,0:T(1,128)S(1)} all-reduce(f32[1,32]{1,0:T(1,128)S(1)} %bitcast.110), channel_id=1, replica_groups=mesh['segment'=8,'rows'=16,'dp'=4] {'rows'}, use_global_device_ids=true, to_apply=%region_3.3 | all-reduce | flops 32 | bytes 256 | tf_op jit(solution)/shard_map/while/body/eval_jaxpr/psum | solution.py:40
  204.5 28.3 %psum.41 = f32[1,32]{1,0:T(1,128)S(1)} all-reduce(f32[1,32]{1,0:T(1,128)S(1)} %bitcast.109), channel_id=1, replica_groups=mesh['segment'=8,'rows'=16,'dp'=4] {'rows'}, use_global_device_ids=true, to_apply=%region_6.6 | all-reduce | flops 32 | bytes 256 | tf_op jit(solution)/shard_map/while/body/eval_jaxpr/psum | solution.py:43
  251.8 29.3 %psum.40 = f32[1,32]{1,0:T(1,128)S(1)} all-reduce(f32[1,32]{1,0:T(1,128)S(1)} %bitcast.110), channel_id=1, replica_groups=mesh['segment'=8,'rows'=16,'dp'=4] {'rows'}, use_global_device_ids=true, to_apply=%region_3.3 | all-reduce | flops 32 | bytes 256 | tf_op jit(solution)/shard_map/while/body/eval_jaxpr/psum | solution.py:40
  282.3 29.0 %psum.41 = f32[1,32]{1,0:T(1,128)S(1)} all-reduce(f32[1,32]{1,0:T(1,128)S(1)} %bitcast.109), channel_id=1, replica_groups=mesh['segment'=8,'rows'=16,'dp'=4] {'rows'}, use_global_device_ids=true, to_apply=%region_6.6 | all-reduce | flops 32 | bytes 256 | tf_op jit(solution)/shard_map/while/body/eval_jaxpr/psum | solution.py:43
  330.4 29.3 %psum.40 = f32[1,32]{1,0:T(1,128)S(1)} all-reduce(f32[1,32]{1,0:T(1,128)S(1)} %bitcast.110), channel_id=1, replica_groups=mesh['segment'=8,'rows'=16,'dp'=4] {'rows'}, use_global_device_ids=true, to_apply=%region_3.3 | all-reduce | flops 32 | bytes 256 | tf_op jit(solution)/shard_map/while/body/eval_jaxpr/psum | solution.py:40
  360.9 28.2 %psum.41 = f32[1,32]{1,0:T(1,128)S(1)} all-reduce(f32[1,32]{1,0:T(1,128)S(1)} %bitcast.109), channel_id=1, replica_groups=mesh['segment'=8,'rows'=16,'dp'=4] {'rows'}, use_global_device_ids=true, to_apply=%region_6.6 | all-reduce | flops 32 | bytes 256 | tf_op jit(solution)/shard_map/while/body/eval_jaxpr/psum | solution.py:43
  408.3 29.3 %psum.40 = f32[1,32]{1,0:T(1,128)S(1)} all-reduce(f32[1,32]{1,0:T(1,128)S(1)} %bitcast.110), channel_id=1, replica_groups=mesh['segment'=8,'rows'=16,'dp'=4] {'rows'}, use_global_device_ids=true, to_apply=%region_3.3 | all-reduce | flops 32 | bytes 256 | tf_op jit(solution)/shard_map/while/body/eval_jaxpr/psum | solution.py:40
  438.8 29.0 %psum.41 = f32[1,32]{1,0:T(1,128)S(1)} all-reduce(f32[1,32]{1,0:T(1,128)S(1)} %bitcast.109), channel_id=1, replica_groups=mesh['segment'=8,'rows'=16,'dp'=4] {'rows'}, use_global_device_ids=true, to_apply=%region_6.6 | all-reduce | flops 32 | bytes 256 | tf_op jit(solution)/shard_map/while/body/eval_jaxpr/psum | solution.py:43
  486.9 29.3 %psum.40 = f32[1,32]{1,0:T(1,128)S(1)} all-reduce(f32[1,32]{1,0:T(1,128)S(1)} %bitcast.110), channel_id=1, replica_groups=mesh['segment'=8,'rows'=16,'dp'=4] {'rows'}, use_global_device_ids=true, to_apply=%region_3.3 | all-reduce | flops 32 | bytes 256 | tf_op jit(solution)/shard_map/while/body/eval_jaxpr/psum | solution.py:40
  517.4 28.2 %psum.41 = f32[1,32]{1,0:T(1,128)S(1)} all-reduce(f32[1,32]{1,0:T(1,128)S(1)} %bitcast.109), channel_id=1, replica_groups=mesh['segment'=8,'rows'=16,'dp'=4] {'rows'}, use_global_device_ids=true, to_apply=%region_6.6 | all-reduce | flops 32 | bytes 256 | tf_op jit(solution)/shard_map/while/body/eval_jaxpr/psum | solution.py:43
  564.7 29.3 %psum.40 = f32[1,32]{1,0:T(1,128)S(1)} all-reduce(f32[1,32]{1,0:T(1,128)S(1)} %bitcast.110), channel_id=1, replica_groups=mesh['segment'=8,'rows'=16,'dp'=4] {'rows'}, use_global_device_ids=true, to_apply=%region_3.3 | all-reduce | flops 32 | bytes 256 | tf_op jit(solution)/shard_map/while/body/eval_jaxpr/psum | solution.py:40
  595.2 29.0 %psum.41 = f32[1,32]{1,0:T(1,128)S(1)} all-reduce(f32[1,32]{1,0:T(1,128)S(1)} %bitcast.109), channel_id=1, replica_groups=mesh['segment'=8,'rows'=16,'dp'=4] {'rows'}, use_global_device_ids=true, to_apply=%region_6.6 | all-reduce | flops 32 | bytes 256 | tf_op jit(solution)/shard_map/while/body/eval_jaxpr/psum | solution.py:43
  643.3 29.3 %psum.40 = f32[1,32]{1,0:T(1,128)S(1)} all-reduce(f32[1,32]{1,0:T(1,128)S(1)} %bitcast.110), channel_id=1, replica_groups=mesh['segment'=8,'rows'=16,'dp'=4] {'rows'}, use_global_device_ids=true, to_apply=%region_3.3 | all-reduce | flops 32 | bytes 256 | tf_op jit(solution)/shard_map/while/body/eval_jaxpr/psum | solution.py:40
  673.8 28.2 %psum.41 = f32[1,32]{1,0:T(1,128)S(1)} all-reduce(f32[1,32]{1,0:T(1,128)S(1)} %bitcast.109), channel_id=1, replica_groups=mesh['segment'=8,'rows'=16,'dp'=4] {'rows'}, use_global_device_ids=true, to_apply=%region_6.6 | all-reduce | flops 32 | bytes 256 | tf_op jit(solution)/shard_map/while/body/eval_jaxpr/psum | solution.py:43
  721.1 29.3 %psum.40 = f32[1,32]{1,0:T(1,128)S(1)} all-reduce(f32[1,32]{1,0:T(1,128)S(1)} %bitcast.110), channel_id=1, replica_groups=mesh['segment'=8,'rows'=16,'dp'=4] {'rows'}, use_global_device_ids=true, to_apply=%region_3.3 | all-reduce | flops 32 | bytes 256 | tf_op jit(solution)/shard_map/while/body/eval_jaxpr/psum | solution.py:40
  751.6 29.0 %psum.41 = f32[1,32]{1,0:T(1,128)S(1)} all-reduce(f32[1,32]{1,0:T(1,128)S(1)} %bitcast.109), channel_id=1, replica_groups=mesh['segment'=8,'rows'=16,'dp'=4] {'rows'}, use_global_device_ids=true, to_apply=%region_6.6 | all-reduce | flops 32 | bytes 256 | tf_op jit(solution)/shard_map/while/body/eval_jaxpr/psum | solution.py:43
  799.7 29.3 %psum.40 = f32[1,32]{1,0:T(1,128)S(1)} all-reduce(f32[1,32]{1,0:T(1,128)S(1)} %bitcast.110), channel_id=1, replica_groups=mesh['segment'=8,'rows'=16,'dp'=4] {'rows'}, use_global_device_ids=true, to_apply=%region_3.3 | all-reduce | flops 32 | bytes 256 | tf_op jit(solution)/shard_map/while/body/eval_jaxpr/psum | solution.py:40
  830.2 28.2 %psum.41 = f32[1,32]{1,0:T(1,128)S(1)} all-reduce(f32[1,32]{1,0:T(1,128)S(1)} %bitcast.109), channel_id=1, replica_groups=mesh['segment'=8,'rows'=16,'dp'=4] {'rows'}, use_global_device_ids=true, to_apply=%region_6.6 | all-reduce | flops 32 | bytes 256 | tf_op jit(solution)/shard_map/while/body/eval_jaxpr/psum | solution.py:43
  875.8 275.4 %all-reduce.3.cloned.1.call-done = f32[3456,128]{1,0:T(8,128)} async-done(((f32[3456,128]{1,0:T(8,128)}), f32[3456,128]{1,0:T(8,128)}) %all-reduce.3.cloned.1.call-update) | async-done | bytes 1769488 | tf_op jit(solution)/shard_map/psum | solution.py:125
  (714 shorter events, 216.9 us)
Async XLA Ops:
  7.2 1144.0 %all-reduce.3.cloned.1.call-start = ((), (), s32[]{:S(2)}) async-start(), calls=%async_computation | async-start | bytes 3538944 | tf_op jit(solution)/shard_map/psum | solution.py:125
  76.0 6.5 collective-permute-start
  77.3 5.9 collective-permute-start.1
  85.6 5.6 collective-permute-start.2
  155.9 6.5 collective-permute-start
  157.2 5.9 collective-permute-start.1
  233.7 6.5 collective-permute-start
  235.0 5.9 collective-permute-start.1
  312.3 6.5 collective-permute-start
  313.6 5.9 collective-permute-start.1
  390.1 6.5 collective-permute-start
  391.4 5.9 collective-permute-start.1
  468.7 6.5 collective-permute-start
  470.0 5.9 collective-permute-start.1
  546.6 6.5 collective-permute-start
  547.9 5.9 collective-permute-start.1
  625.2 6.5 collective-permute-start
  626.5 5.9 collective-permute-start.1
  703.0 6.5 collective-permute-start
  704.3 5.9 collective-permute-start.1
  781.6 6.5 collective-permute-start
  782.9 5.9 collective-permute-start.1
  859.4 6.5 collective-permute-start
  860.7 5.9 collective-permute-start.1
  (56 other events, 377.8 us)
Sparse Core Ops, SparseCore 0:
  875.9 275.2 all-reduce.2
where the time goes:
time: 1160 us
  blocking collectives  644 us (56%)
  waiting for transfers between devices  299 us (26%)
  starting transfers between devices  85.4 us (7%)
  other arithmetic  58.3 us (5%)
  matrix products  32.1 us (3%)
  local copies, waits for them, and re-layouts  17.7 us (2%)
  between operations  14.1 us (1%)
    psum x11, blocking collectives, statistics(): total = lax.psum(jnp.sum(grouped * mask_six, axis=(1, 2, 3, 5)), 'rows')  331 us
    psum x11, blocking collectives, statistics(): lax.psum(jnp.sum(centered * centered * mask_six, axis=(1, 2, 3, 5)), 'rows')  313 us
    psum x1, waiting for transfers between devices, per_device(): grads = lax.psum(grads, ('rows', 'dp')) * factor  275 us
    ppermute x11, starting transfers between devices, extended_2(): lax.ppermute(tail, axis, [(i, (i + 1) % count) for i in range(ends)])  50 us
    dot_general x11, matrix products, tick(): lax.dot_general(patches, masked, (((0,), (0,)), ((), ())), preferred_elem...  24.9 us
  transfers between devices with their start and end apart: 34, of which 23 were waited for; matrix products, arithmetic and copies ran while one was open for 3% of the time, Pallas kernels for 0%

commit v1 on v0

--- a/solution.py
+++ b/solution.py
@@ -3,6 +3,7 @@
 import jax.numpy as jnp
 from jax import lax
 from jax.sharding import PartitionSpec as P
+from jax.lax import psum
 
 GROUPS = 32
 eps = 1e-06
@@ -122,7 +123,7 @@
         jnp.zeros((27 * chans, chans), jnp.float32),
     )
     arrived, stash, grads = lax.fori_loop(0, micro + segments - 1, tick, start)
-    grads = lax.psum(grads, ("rows", "dp")) * factor
+    grads = psum(psum(grads, "rows"), "dp") * factor
     return (stash[None], grads[None])
 
 

time: 1160 us -> 1100 us (0.948)
  the two profiles are of different devices: /device:TPU:8 before, /device:TPU:1 now
where the time goes in v1:
time: 1100 us; the launch traced here: 1090 us
  blocking collectives  490 us (45%)
  starting transfers between devices  262 us (24%)
  waiting for transfers between devices  210 us (19%)
  other arithmetic  58.4 us (5%)
  matrix products  32.1 us (3%)
  local copies, waits for them, and re-layouts  17.7 us (2%)
  between operations  14.1 us (1%)
    psum x11, blocking collectives, statistics(): total = lax.psum(jnp.sum(grouped * mask_six, axis=(1, 2, 3, 5)), 'rows')  254 us
    psum x11, blocking collectives, statistics(): lax.psum(jnp.sum(centered * centered * mask_six, axis=(1, 2, 3, 5)), 'rows')  237 us
    psum x2, waiting for transfers between devices, per_device(): grads = psum(psum(grads, 'rows'), 'dp') * factor  208 us
    ppermute x11, starting transfers between devices, passed_along(): return lax.ppermute(block, axis, route)  204 us
    ppermute x11, starting transfers between devices, extended_2(): lax.ppermute(tail, axis, [(i, (i + 1) % count) for i in range(ends)])  43.8 us
    dot_general x11, matrix products, tick(): lax.dot_general(patches, masked, (((0,), (0,)), ((), ())), preferred_elem...  24.9 us
  transfers between devices with their start and end apart: 35, of which 13 were waited for; matrix products, arithmetic and copies ran while one was open for 3% of the time, Pallas kernels for 0%

profile of v1, /device:TPU:1, one launch (start us, length us, event | category | flops | bytes accessed | tf_op | source)
XLA Modules:
  0.0 1094.8 jit_solution(16454320395352553816)
XLA Ops:
  7.3 868.5 %while.20 = (s32[]{:T(128)}, bf16[1,4,8,8,128]{4,3,2,1,0:T(8,128)(2,1)S(1)}, bf16[4,1,4,8,8,128]{5,4,3,2,1,0:T(8,128)(2,1)S(1)}, f32[3456,128]{1,0:T(8,128)S(1)}...) while((s32[]{:T(128)}, ...), condition=%wide.region_7.8_spmd.clone, body=%wide.region_0.7_spmd.clone.sunk | while | flops 457701504 | bytes 18060908 | solution.py:125
  10.4 30.3 %psum.48 = f32[1,32]{1,0:T(1,128)S(1)} all-reduce(f32[1,32]{1,0:T(1,128)S(1)} %bitcast.110), channel_id=1, replica_groups=mesh['segment'=8,'rows'=16,'dp'=4] {'rows'}, use_global_device_ids=true, to_apply=%region_3.3 | all-reduce | flops 32 | bytes 256 | tf_op jit(solution)/shard_map/while/body/eval_jaxpr/psum | solution.py:41
  95.5 23.3 %psum.48 = f32[1,32]{1,0:T(1,128)S(1)} all-reduce(f32[1,32]{1,0:T(1,128)S(1)} %bitcast.110), channel_id=1, replica_groups=mesh['segment'=8,'rows'=16,'dp'=4] {'rows'}, use_global_device_ids=true, to_apply=%region_3.3 | all-reduce | flops 32 | bytes 256 | tf_op jit(solution)/shard_map/while/body/eval_jaxpr/psum | solution.py:41
  119.9 22.4 %psum.49 = f32[1,32]{1,0:T(1,128)S(1)} all-reduce(f32[1,32]{1,0:T(1,128)S(1)} %bitcast.109), channel_id=1, replica_groups=mesh['segment'=8,'rows'=16,'dp'=4] {'rows'}, use_global_device_ids=true, to_apply=%region_6.6 | all-reduce | flops 32 | bytes 256 | tf_op jit(solution)/shard_map/while/body/eval_jaxpr/psum | solution.py:44
  175.3 22.1 %psum.48 = f32[1,32]{1,0:T(1,128)S(1)} all-reduce(f32[1,32]{1,0:T(1,128)S(1)} %bitcast.110), channel_id=1, replica_groups=mesh['segment'=8,'rows'=16,'dp'=4] {'rows'}, use_global_device_ids=true, to_apply=%region_3.3 | all-reduce | flops 32 | bytes 256 | tf_op jit(solution)/shard_map/while/body/eval_jaxpr/psum | solution.py:41
  198.6 21.5 %psum.49 = f32[1,32]{1,0:T(1,128)S(1)} all-reduce(f32[1,32]{1,0:T(1,128)S(1)} %bitcast.109), channel_id=1, replica_groups=mesh['segment'=8,'rows'=16,'dp'=4] {'rows'}, use_global_device_ids=true, to_apply=%region_6.6 | all-reduce | flops 32 | bytes 256 | tf_op jit(solution)/shard_map/while/body/eval_jaxpr/psum | solution.py:44
  253.2 22.4 %psum.48 = f32[1,32]{1,0:T(1,128)S(1)} all-reduce(f32[1,32]{1,0:T(1,128)S(1)} %bitcast.110), channel_id=1, replica_groups=mesh['segment'=8,'rows'=16,'dp'=4] {'rows'}, use_global_device_ids=true, to_apply=%region_3.3 | all-reduce | flops 32 | bytes 256 | tf_op jit(solution)/shard_map/while/body/eval_jaxpr/psum | solution.py:41
  276.7 22.0 %psum.49 = f32[1,32]{1,0:T(1,128)S(1)} all-reduce(f32[1,32]{1,0:T(1,128)S(1)} %bitcast.109), channel_id=1, replica_groups=mesh['segment'=8,'rows'=16,'dp'=4] {'rows'}, use_global_device_ids=true, to_apply=%region_6.6 | all-reduce | flops 32 | bytes 256 | tf_op jit(solution)/shard_map/while/body/eval_jaxpr/psum | solution.py:44
  331.8 22.3 %psum.48 = f32[1,32]{1,0:T(1,128)S(1)} all-reduce(f32[1,32]{1,0:T(1,128)S(1)} %bitcast.110), channel_id=1, replica_groups=mesh['segment'=8,'rows'=16,'dp'=4] {'rows'}, use_global_device_ids=true, to_apply=%region_3.3 | all-reduce | flops 32 | bytes 256 | tf_op jit(solution)/shard_map/while/body/eval_jaxpr/psum | solution.py:41
  355.3 21.6 %psum.49 = f32[1,32]{1,0:T(1,128)S(1)} all-reduce(f32[1,32]{1,0:T(1,128)S(1)} %bitcast.109), channel_id=1, replica_groups=mesh['segment'=8,'rows'=16,'dp'=4] {'rows'}, use_global_device_ids=true, to_apply=%region_6.6 | all-reduce | flops 32 | bytes 256 | tf_op jit(solution)/shard_map/while/body/eval_jaxpr/psum | solution.py:44
  409.6 22.2 %psum.48 = f32[1,32]{1,0:T(1,128)S(1)} all-reduce(f32[1,32]{1,0:T(1,128)S(1)} %bitcast.110), channel_id=1, replica_groups=mesh['segment'=8,'rows'=16,'dp'=4] {'rows'}, use_global_device_ids=true, to_apply=%region_3.3 | all-reduce | flops 32 | bytes 256 | tf_op jit(solution)/shard_map/while/body/eval_jaxpr/psum | solution.py:41
  433.0 21.8 %psum.49 = f32[1,32]{1,0:T(1,128)S(1)} all-reduce(f32[1,32]{1,0:T(1,128)S(1)} %bitcast.109), channel_id=1, replica_groups=mesh['segment'=8,'rows'=16,'dp'=4] {'rows'}, use_global_device_ids=true, to_apply=%region_6.6 | all-reduce | flops 32 | bytes 256 | tf_op jit(solution)/shard_map/while/body/eval_jaxpr/psum | solution.py:44
  488.2 22.2 %psum.48 = f32[1,32]{1,0:T(1,128)S(1)} all-reduce(f32[1,32]{1,0:T(1,128)S(1)} %bitcast.110), channel_id=1, replica_groups=mesh['segment'=8,'rows'=16,'dp'=4] {'rows'}, use_global_device_ids=true, to_apply=%region_3.3 | all-reduce | flops 32 | bytes 256 | tf_op jit(solution)/shard_map/while/body/eval_jaxpr/psum | solution.py:41
  511.5 20.9 %psum.49 = f32[1,32]{1,0:T(1,128)S(1)} all-reduce(f32[1,32]{1,0:T(1,128)S(1)} %bitcast.109), channel_id=1, replica_groups=mesh['segment'=8,'rows'=16,'dp'=4] {'rows'}, use_global_device_ids=true, to_apply=%region_6.6 | all-reduce | flops 32 | bytes 256 | tf_op jit(solution)/shard_map/while/body/eval_jaxpr/psum | solution.py:44
  566.0 22.1 %psum.48 = f32[1,32]{1,0:T(1,128)S(1)} all-reduce(f32[1,32]{1,0:T(1,128)S(1)} %bitcast.110), channel_id=1, replica_groups=mesh['segment'=8,'rows'=16,'dp'=4] {'rows'}, use_global_device_ids=true, to_apply=%region_3.3 | all-reduce | flops 32 | bytes 256 | tf_op jit(solution)/shard_map/while/body/eval_jaxpr/psum | solution.py:41
  589.3 22.3 %psum.49 = f32[1,32]{1,0:T(1,128)S(1)} all-reduce(f32[1,32]{1,0:T(1,128)S(1)} %bitcast.109), channel_id=1, replica_groups=mesh['segment'=8,'rows'=16,'dp'=4] {'rows'}, use_global_device_ids=true, to_apply=%region_6.6 | all-reduce | flops 32 | bytes 256 | tf_op jit(solution)/shard_map/while/body/eval_jaxpr/psum | solution.py:44
  644.6 22.3 %psum.48 = f32[1,32]{1,0:T(1,128)S(1)} all-reduce(f32[1,32]{1,0:T(1,128)S(1)} %bitcast.110), channel_id=1, replica_groups=mesh['segment'=8,'rows'=16,'dp'=4] {'rows'}, use_global_device_ids=true, to_apply=%region_3.3 | all-reduce | flops 32 | bytes 256 | tf_op jit(solution)/shard_map/while/body/eval_jaxpr/psum | solution.py:41
  668.1 21.1 %psum.49 = f32[1,32]{1,0:T(1,128)S(1)} all-reduce(f32[1,32]{1,0:T(1,128)S(1)} %bitcast.109), channel_id=1, replica_groups=mesh['segment'=8,'rows'=16,'dp'=4] {'rows'}, use_global_device_ids=true, to_apply=%region_6.6 | all-reduce | flops 32 | bytes 256 | tf_op jit(solution)/shard_map/while/body/eval_jaxpr/psum | solution.py:44
  722.5 22.4 %psum.48 = f32[1,32]{1,0:T(1,128)S(1)} all-reduce(f32[1,32]{1,0:T(1,128)S(1)} %bitcast.110), channel_id=1, replica_groups=mesh['segment'=8,'rows'=16,'dp'=4] {'rows'}, use_global_device_ids=true, to_apply=%region_3.3 | all-reduce | flops 32 | bytes 256 | tf_op jit(solution)/shard_map/while/body/eval_jaxpr/psum | solution.py:41
  746.0 21.8 %psum.49 = f32[1,32]{1,0:T(1,128)S(1)} all-reduce(f32[1,32]{1,0:T(1,128)S(1)} %bitcast.109), channel_id=1, replica_groups=mesh['segment'=8,'rows'=16,'dp'=4] {'rows'}, use_global_device_ids=true, to_apply=%region_6.6 | all-reduce | flops 32 | bytes 256 | tf_op jit(solution)/shard_map/while/body/eval_jaxpr/psum | solution.py:44
  801.1 22.2 %psum.48 = f32[1,32]{1,0:T(1,128)S(1)} all-reduce(f32[1,32]{1,0:T(1,128)S(1)} %bitcast.110), channel_id=1, replica_groups=mesh['segment'=8,'rows'=16,'dp'=4] {'rows'}, use_global_device_ids=true, to_apply=%region_3.3 | all-reduce | flops 32 | bytes 256 | tf_op jit(solution)/shard_map/while/body/eval_jaxpr/psum | solution.py:41
  824.5 21.2 %psum.49 = f32[1,32]{1,0:T(1,128)S(1)} all-reduce(f32[1,32]{1,0:T(1,128)S(1)} %bitcast.109), channel_id=1, replica_groups=mesh['segment'=8,'rows'=16,'dp'=4] {'rows'}, use_global_device_ids=true, to_apply=%region_6.6 | all-reduce | flops 32 | bytes 256 | tf_op jit(solution)/shard_map/while/body/eval_jaxpr/psum | solution.py:44
  877.1 131.2 %all-reduce.4.cloned.1.call-done = f32[3456,128]{1,0:T(8,128)} async-done(((f32[3456,128]{1,0:T(8,128)}), f32[3456,128]{1,0:T(8,128)}) %all-reduce.4.cloned.1.call-update) | async-done | bytes 1769488 | tf_op jit(solution)/shard_map/psum | solution.py:126
  1008.4 76.8 %all-reduce.6.cloned.1.call-done = f32[3456,128]{1,0:T(8,128)} async-done(((f32[3456,128]{1,0:T(8,128)}), f32[3456,128]{1,0:T(8,128)}) %all-reduce.6.cloned.1.call-update) | async-done | bytes 1769488 | tf_op jit(solution)/shard_map/psum | solution.py:126
  (717 shorter events, 391.8 us)
Async XLA Ops:
  7.2 1001.2 %all-reduce.4.cloned.1.call-start = ((), (), s32[]{:S(2)}) async-start(), calls=%async_computation | async-start | bytes 3538944 | tf_op jit(solution)/shard_map/psum | solution.py:126
  62.9 5.9 collective-permute-start
  71.3 21.1 %collective-permute-start.2 = (bf16[1,4,8,8,128]{4,3,2,1,0:T(8,128)(2,1)S(1)}, bf16[1,4,8,8,128]{4,3,2,1,0:T(8,128)(2,1)S(1)}, u32[]{:S(2)}, u32[]{:S(2)}) collective-permute-start(bf16[1,4,8,8,128]{4,3,2,1,0:T(8,128)(2,1)S(1)} %get-tuple-element.466), channel_id=1, source_target_pairs={{0,64},{64,128},{128,192},{192,256},{256,320},{320,384},{384,448},... | collective-permute-start | bytes 196616 | tf_op jit(solution)/shard_map/while/body/eval_jaxpr/ppermute | solution.py:32
  143.3 5.9 collective-permute-start
  151.7 20.6 %collective-permute-start.2 = (bf16[1,4,8,8,128]{4,3,2,1,0:T(8,128)(2,1)S(1)}, bf16[1,4,8,8,128]{4,3,2,1,0:T(8,128)(2,1)S(1)}, u32[]{:S(2)}, u32[]{:S(2)}) collective-permute-start(bf16[1,4,8,8,128]{4,3,2,1,0:T(8,128)(2,1)S(1)} %get-tuple-element.466), channel_id=1, source_target_pairs={{0,64},{64,128},{128,192},{192,256},{256,320},{320,384},{384,448},... | collective-permute-start | bytes 196616 | tf_op jit(solution)/shard_map/while/body/eval_jaxpr/ppermute | solution.py:32
  221.0 5.9 collective-permute-start
  229.4 20.7 %collective-permute-start.2 = (bf16[1,4,8,8,128]{4,3,2,1,0:T(8,128)(2,1)S(1)}, bf16[1,4,8,8,128]{4,3,2,1,0:T(8,128)(2,1)S(1)}, u32[]{:S(2)}, u32[]{:S(2)}) collective-permute-start(bf16[1,4,8,8,128]{4,3,2,1,0:T(8,128)(2,1)S(1)} %get-tuple-element.466), channel_id=1, source_target_pairs={{0,64},{64,128},{128,192},{192,256},{256,320},{320,384},{384,448},... | collective-permute-start | bytes 196616 | tf_op jit(solution)/shard_map/while/body/eval_jaxpr/ppermute | solution.py:32
  299.6 5.9 collective-permute-start
  308.0 20.7 %collective-permute-start.2 = (bf16[1,4,8,8,128]{4,3,2,1,0:T(8,128)(2,1)S(1)}, bf16[1,4,8,8,128]{4,3,2,1,0:T(8,128)(2,1)S(1)}, u32[]{:S(2)}, u32[]{:S(2)}) collective-permute-start(bf16[1,4,8,8,128]{4,3,2,1,0:T(8,128)(2,1)S(1)} %get-tuple-element.466), channel_id=1, source_target_pairs={{0,64},{64,128},{128,192},{192,256},{256,320},{320,384},{384,448},... | collective-permute-start | bytes 196616 | tf_op jit(solution)/shard_map/while/body/eval_jaxpr/ppermute | solution.py:32
  377.9 5.9 collective-permute-start
  386.3 20.3 %collective-permute-start.2 = (bf16[1,4,8,8,128]{4,3,2,1,0:T(8,128)(2,1)S(1)}, bf16[1,4,8,8,128]{4,3,2,1,0:T(8,128)(2,1)S(1)}, u32[]{:S(2)}, u32[]{:S(2)}) collective-permute-start(bf16[1,4,8,8,128]{4,3,2,1,0:T(8,128)(2,1)S(1)} %get-tuple-element.466), channel_id=1, source_target_pairs={{0,64},{64,128},{128,192},{192,256},{256,320},{320,384},{384,448},... | collective-permute-start | bytes 196616 | tf_op jit(solution)/shard_map/while/body/eval_jaxpr/ppermute | solution.py:32
  455.7 5.9 collective-permute-start
  464.1 21.0 %collective-permute-start.2 = (bf16[1,4,8,8,128]{4,3,2,1,0:T(8,128)(2,1)S(1)}, bf16[1,4,8,8,128]{4,3,2,1,0:T(8,128)(2,1)S(1)}, u32[]{:S(2)}, u32[]{:S(2)}) collective-permute-start(bf16[1,4,8,8,128]{4,3,2,1,0:T(8,128)(2,1)S(1)} %get-tuple-element.466), channel_id=1, source_target_pairs={{0,64},{64,128},{128,192},{192,256},{256,320},{320,384},{384,448},... | collective-permute-start | bytes 196616 | tf_op jit(solution)/shard_map/while/body/eval_jaxpr/ppermute | solution.py:32
  533.4 5.9 collective-permute-start
  541.8 21.2 %collective-permute-start.2 = (bf16[1,4,8,8,128]{4,3,2,1,0:T(8,128)(2,1)S(1)}, bf16[1,4,8,8,128]{4,3,2,1,0:T(8,128)(2,1)S(1)}, u32[]{:S(2)}, u32[]{:S(2)}) collective-permute-start(bf16[1,4,8,8,128]{4,3,2,1,0:T(8,128)(2,1)S(1)} %get-tuple-element.466), channel_id=1, source_target_pairs={{0,64},{64,128},{128,192},{192,256},{256,320},{320,384},{384,448},... | collective-permute-start | bytes 196616 | tf_op jit(solution)/shard_map/while/body/eval_jaxpr/ppermute | solution.py:32
  612.5 5.9 collective-permute-start
  620.9 20.7 %collective-permute-start.2 = (bf16[1,4,8,8,128]{4,3,2,1,0:T(8,128)(2,1)S(1)}, bf16[1,4,8,8,128]{4,3,2,1,0:T(8,128)(2,1)S(1)}, u32[]{:S(2)}, u32[]{:S(2)}) collective-permute-start(bf16[1,4,8,8,128]{4,3,2,1,0:T(8,128)(2,1)S(1)} %get-tuple-element.466), channel_id=1, source_target_pairs={{0,64},{64,128},{128,192},{192,256},{256,320},{320,384},{384,448},... | collective-permute-start | bytes 196616 | tf_op jit(solution)/shard_map/while/body/eval_jaxpr/ppermute | solution.py:32
  690.2 5.9 collective-permute-start
  698.6 20.8 %collective-permute-start.2 = (bf16[1,4,8,8,128]{4,3,2,1,0:T(8,128)(2,1)S(1)}, bf16[1,4,8,8,128]{4,3,2,1,0:T(8,128)(2,1)S(1)}, u32[]{:S(2)}, u32[]{:S(2)}) collective-permute-start(bf16[1,4,8,8,128]{4,3,2,1,0:T(8,128)(2,1)S(1)} %get-tuple-element.466), channel_id=1, source_target_pairs={{0,64},{64,128},{128,192},{192,256},{256,320},{320,384},{384,448},... | collective-permute-start | bytes 196616 | tf_op jit(solution)/shard_map/while/body/eval_jaxpr/ppermute | solution.py:32
  768.7 5.9 collective-permute-start
  777.1 20.9 %collective-permute-start.2 = (bf16[1,4,8,8,128]{4,3,2,1,0:T(8,128)(2,1)S(1)}, bf16[1,4,8,8,128]{4,3,2,1,0:T(8,128)(2,1)S(1)}, u32[]{:S(2)}, u32[]{:S(2)}) collective-permute-start(bf16[1,4,8,8,128]{4,3,2,1,0:T(8,128)(2,1)S(1)} %get-tuple-element.466), channel_id=1, source_target_pairs={{0,64},{64,128},{128,192},{192,256},{256,320},{320,384},{384,448},... | collective-permute-start | bytes 196616 | tf_op jit(solution)/shard_map/while/body/eval_jaxpr/ppermute | solution.py:32
  846.6 5.9 collective-permute-start
  855.0 20.8 %collective-permute-start.2 = (bf16[1,4,8,8,128]{4,3,2,1,0:T(8,128)(2,1)S(1)}, bf16[1,4,8,8,128]{4,3,2,1,0:T(8,128)(2,1)S(1)}, u32[]{:S(2)}, u32[]{:S(2)}) collective-permute-start(bf16[1,4,8,8,128]{4,3,2,1,0:T(8,128)(2,1)S(1)} %get-tuple-element.466), channel_id=1, source_target_pairs={{0,64},{64,128},{128,192},{192,256},{256,320},{320,384},{384,448},... | collective-permute-start | bytes 196616 | tf_op jit(solution)/shard_map/while/body/eval_jaxpr/ppermute | solution.py:32
  877.1 208.0 %all-reduce.6.cloned.1.call-start = ((), (), s32[]{:S(2)}) async-start(), calls=%async_computation.1 | async-start | bytes 3538944 | tf_op jit(solution)/shard_map/psum | solution.py:126
  (57 other events, 227.5 us)
Sparse Core Ops, SparseCore 0:
  877.2 131.0 all-reduce.3
  1010.8 74.2 all-reduce.5
